TPU v7x, 1024 devices: a whole 8x8x8 slice. The times are simulated.
1024 devices in a mesh: dp: 128 (over x, y, core), tensor: 8 (over z).
Axes of the slice: x: 8, y: 8, z: 8, core: 2. Of those that a mesh axis runs over, the one named last changes fastest.
Arguments:
- tokens: bfloat16 [16384, 8192], P('dp', 'tensor'), may hold values from -6 to 6
- kv_weight: bfloat16 [8192, 2048], P('tensor'), may hold values from -0.0625 to 0.0625
- adapter_down: bfloat16 [512, 8, 1024, 32], P(None, 'tensor', 'dp'), may hold values from -0.0625 to 0.0625
- adapter_up: bfloat16 [512, 32, 8, 256], P(None, None, 'tensor', 'dp'), may hold values from -1 to 1
- cotangent: bfloat16 [16384, 2048], P('dp'), may hold values from -1.5 to 1.5
- block_adapter: int32 [128], replicated, may hold values from 0 to 511
- block_rows: int32 [128], P('dp'), may hold values from 32 to 128
Outputs:
- key_value_output: bfloat16 [16384, 2048], P('dp', 'tensor')
- token_gradient: bfloat16 [16384, 8192], P('dp', 'tensor')
- grad_down: float32 [512, 8, 1024, 32], P(None, 'tensor', 'dp')
- grad_up: float32 [512, 32, 8, 256], P(None, None, 'tensor', 'dp')
Inputs may be any that keep to these rules, and one draw needn't show every extreme that they name: `block_adapter`: block j belongs to the tokens of dp index j; an adapter may serve many blocks or none. `block_rows`: the live rows of a block come first.
All inputs are finite; a program needn't handle non-finite values.
Results may differ from a plain program's by a relative error of at most 0.015.
Values may be sent and summed in bfloat16 or wider, within the bound.
A program may use at most 32 MiB of HBM per device.

v0:
```python
import jax
import jax.numpy as jnp
from jax import lax
from jax.sharding import PartitionSpec as P


def shards(tokens, kv_weight, adapter_down, adapter_up, cotangent, block_adapter, block_rows):
    groups = lax.axis_size("dp")
    tensor_parts = lax.axis_size("tensor")
    column = lax.axis_index("tensor")
    count_of_blocks = block_rows.shape[0]
    block_length = tokens.shape[0] // count_of_blocks
    feature_width = tokens.shape[1]
    n_adapters = adapter_down.shape[0]
    slice_rows = adapter_down.shape[2]
    rank_width = adapter_down.shape[3]
    slice_cols = adapter_up.shape[3]
    kv_width = kv_weight.shape[1]
    column_width = kv_width // tensor_parts
    ids_send = block_adapter.reshape(groups, count_of_blocks).T
    down_table = adapter_down.reshape(n_adapters, slice_rows * rank_width)
    up_table = adapter_up.reshape(n_adapters, rank_width * slice_cols)
    down_recv, up_recv = (
        lax.all_to_all(down_table[ids_send], "dp", split_axis=1, concat_axis=1, tiled=True),
        lax.all_to_all(up_table[ids_send], "dp", split_axis=1, concat_axis=1, tiled=True),
    )
    local_down_weight = down_recv.reshape(count_of_blocks, feature_width, rank_width)
    local_up_weight = up_recv.reshape(count_of_blocks, groups, rank_width, slice_cols).transpose(
        0, 2, 1, 3
    )
    local_up_weight = local_up_weight.reshape(count_of_blocks, rank_width, column_width)
    live_rows = jnp.arange(block_length, dtype=jnp.int32)[None, :] < block_rows[:, None]
    row_selection_mask = live_rows.astype(jnp.bfloat16).reshape(count_of_blocks * block_length)
    dy_masked = cotangent * row_selection_mask[:, None]
    dy_cols = lax.dynamic_slice_in_dim(dy_masked, column * column_width, column_width, 1)
    tok_blocks = tokens.reshape(count_of_blocks, block_length, feature_width)
    dy_blocks = dy_cols.reshape(count_of_blocks, block_length, column_width)
    rank_part = jnp.einsum(
        "bnd,bdr->bnr", tok_blocks, local_down_weight, preferred_element_type=jnp.float32
    )
    back_part = jnp.einsum(
        "bnk,brk->bnr", dy_blocks, local_up_weight, preferred_element_type=jnp.float32
    )
    base_part = jnp.dot(tokens, kv_weight, preferred_element_type=jnp.float32)
    local_frozen_weight = lax.psum_scatter(
        base_part.astype(jnp.bfloat16), "tensor", scatter_dimension=1, tiled=True
    ).astype(jnp.float32)
    rank_sum, back_sum = lax.psum((rank_part, back_part), "tensor")
    rank_activation = rank_sum.astype(jnp.bfloat16)
    rank_gradient = back_sum.astype(jnp.bfloat16)
    adapter_output = jnp.einsum(
        "igu,iul->igl", rank_activation, local_up_weight, preferred_element_type=jnp.float32
    )
    adapter_output = adapter_output.reshape(count_of_blocks * block_length, column_width)
    key_value_output = (
        (local_frozen_weight + adapter_output) * row_selection_mask[:, None].astype(jnp.float32)
    ).astype(jnp.bfloat16)
    backward_frozen_term = lax.dot_general(
        dy_masked, kv_weight, (((1,), (1,)), ((), ())), preferred_element_type=jnp.float32
    )
    backward_adapter_term = jnp.einsum(
        "oxe,oue->oxu", rank_gradient, local_down_weight, preferred_element_type=jnp.float32
    )
    token_gradient = (
        backward_frozen_term
        + backward_adapter_term.reshape(count_of_blocks * block_length, feature_width)
    ).astype(jnp.bfloat16)
    down_terms = jnp.einsum(
        "bnd,bnr->bdr", tok_blocks, rank_gradient, preferred_element_type=jnp.float32
    ).astype(jnp.bfloat16)
    down_terms = down_terms.reshape(count_of_blocks, groups, slice_rows * rank_width)
    up_terms = jnp.einsum(
        "bnr,bnk->brk", rank_activation, dy_blocks, preferred_element_type=jnp.float32
    ).astype(jnp.bfloat16)
    up_terms = up_terms.reshape(count_of_blocks, rank_width, groups, slice_cols).transpose(
        0, 2, 1, 3
    )
    up_terms = up_terms.reshape(count_of_blocks, groups, rank_width * slice_cols)
    down_back, up_back = (
        lax.all_to_all(down_terms, "dp", split_axis=1, concat_axis=1, tiled=True),
        lax.all_to_all(up_terms, "dp", split_axis=1, concat_axis=1, tiled=True),
    )
    owners = jnp.arange(n_adapters, dtype=jnp.int32)
    onehot = (ids_send[None, :, :] == owners[:, None, None]).astype(jnp.bfloat16)
    grad_down = jnp.einsum("abs,bsk->ak", onehot, down_back, preferred_element_type=jnp.float32)
    grad_up = jnp.einsum("abs,bsk->ak", onehot, up_back, preferred_element_type=jnp.float32)
    grad_down = grad_down.reshape(n_adapters, 1, slice_rows, rank_width)
    grad_up = grad_up.reshape(n_adapters, rank_width, 1, slice_cols)
    return (key_value_output, token_gradient, grad_down, grad_up)


def solution(mesh):
    return jax.shard_map(
        shards,
        mesh=mesh,
        in_specs=(
            P("dp", "tensor"),
            P("tensor", None),
            P(None, "tensor", "dp", None),
            P(None, None, "tensor", "dp"),
            P("dp", None),
            P(),
            P("dp"),
        ),
        out_specs=(
            P("dp", "tensor"),
            P("dp", "tensor"),
            P(None, "tensor", "dp", None),
            P(None, None, "tensor", "dp"),
        ),
        check_vma=False,
    )
```

profile of v0, /device:TPU:1, one launch (start us, length us, event | category | flops | bytes accessed | tf_op | source)
XLA Modules:
  0.0 147.3 jit_solution(8461908238152827281)
XLA Ops:
  7.2 0.0 copy-start
  7.2 0.0 copy-start.1
  7.2 0.0 copy-start.2
  7.2 1.0 reshape.171
  8.2 0.1 copy.41
  8.3 0.7 compare_select_fusion
  9.0 0.7 gather_fusion.1
  9.7 0.7 copy.42
  10.3 19.3 %all-to-all-start.1 = ((bf16[1,128,64]{2,0,1:T(2,128)(2,1)}), bf16[1,128,64]{2,0,1:T(2,128)(2,1)S(1)}, u32[]{:S(2)}, u32[]{:S(2)}) async-start(bf16[1,128,64]{2,0,1:T(2,128)(2,1)} %copy.42), calls=%async_computation.2 | async-start | bytes 131072 | tf_op jit(solution)/shard_map/all_to_all | solution.py:25
  29.7 0.0 reduce-scatter.2.cloned.1.call-start
  29.7 0.0 copy-done
  29.7 3.7 %convolution_convert_fusion = bf16[128,2048]{1,0:T(8,128)(2,1)} fusion(bf16[128,1024]{1,0:T(8,128)(2,1)S(1)} %copy-done, bf16[1024,2048]{1,0:T(8,128)(2,1)} %param.8), kind=kOutput, calls=%fused_computation.2 | convolution fusion | flops 537133056 | bytes 4980736 | tf_op jit(solution)/shard_map/dot_general | solution.py:44
  33.4 0.0 reduce-scatter.2.cloned.1.call-update
  34.1 0.0 copy-done.1
  34.1 0.1 broadcast_multiply_fusion
  34.2 0.0 copy-done.2
  34.2 0.1 copy.39
  34.4 0.8 gather_fusion
  35.2 0.1 copy.59
  35.3 0.5 broadcast.53
  35.8 1.0 reduce.2
  36.8 0.7 reshape.203
  37.5 3.8 %all-to-all-done.1 = bf16[1,128,64]{2,0,1:T(2,128)(2,1)S(1)} async-done(((bf16[1,128,64]{2,0,1:T(2,128)(2,1)}), bf16[1,128,64]{2,0,1:T(2,128)(2,1)S(1)}, u32[]{:S(2)}, u32[]{:S(2)}) %all-to-all-start.1) | async-done | bytes 16416 | tf_op jit(solution)/shard_map/all_to_all | solution.py:25
  41.3 10.1 %all-to-all-start = ((bf16[128,2,128]{2,1,0:T(2,128)(2,1)}), bf16[128,2,128]{2,1,0:T(2,128)(2,1)S(1)}, u32[]{:S(2)}, u32[]{:S(2)}) async-start(bf16[128,2,128]{2,1,0:T(2,128)(2,1)} %reshape.203), calls=%async_computation.1 | async-start | bytes 131072 | tf_op jit(solution)/shard_map/all_to_all | solution.py:24
  51.4 0.1 copy.43
  51.5 0.1 copy.44
  51.6 0.2 convolution_bitcast_fusion.2
  51.8 11.0 %all-to-all-done = bf16[128,2,128]{2,1,0:T(2,128)(2,1)S(1)} async-done(((bf16[128,2,128]{2,1,0:T(2,128)(2,1)}), bf16[128,2,128]{2,1,0:T(2,128)(2,1)S(1)}, u32[]{:S(2)}, u32[]{:S(2)}) %all-to-all-start) | async-done | bytes 65568 | tf_op jit(solution)/shard_map/all_to_all | solution.py:24
  62.8 0.4 bitcast_reduce_fusion
  63.2 0.2 reshape.169
  63.4 0.2 convolution_bitcast_fusion.3
  63.6 31.6 %all-reduce = (bf16[1,128,32]{1,2,0:T(8,128)(2,1)S(1)}, bf16[1,128,32]{1,2,0:T(8,128)(2,1)S(1)}) all-reduce(f32[1,128,32]{1,2,0:T(8,128)S(1)} %convolution_bitcast_fusion.3, f32[1,128,32]{1,2,0:T(8,128)S(1)} %convolution_bitcast_fusion.2), channel_id=1, replica_groups=mesh['dp'=128,'tensor'=8] {'tensor'}, use_global_device_ids=true, to_apply=%region_1.0 | all-reduce | flops 8192 | bytes 49152 | tf_op jit(solution)/shard_map/psum | solution.py:48
  95.2 0.0 copy-start.3
  95.2 0.1 convolution_convert_fusion.2
  95.3 0.1 copy.48
  95.4 0.1 copy.49
  95.5 0.8 copy.50
  96.3 12.3 %all-to-all-start.3 = ((bf16[1,128,64]{2,0,1:T(2,128)(2,1)}), bf16[1,128,64]{2,0,1:T(2,128)(2,1)S(1)}, u32[]{:S(2)}, u32[]{:S(2)}) async-start(bf16[1,128,64]{2,0,1:T(2,128)(2,1)} %copy.50), calls=%async_computation.4 | async-start | bytes 131072 | tf_op jit(solution)/shard_map/all_to_all | solution.py:81
  108.6 0.2 fusion.13
  108.9 0.2 fusion.3
  109.0 0.2 copy.45
  109.2 0.2 reshape.201
  109.4 1.0 reduce.3
  110.4 0.7 reshape.205
  111.1 9.2 %all-to-all-done.3 = bf16[1,128,64]{2,0,1:T(2,128)(2,1)S(1)} async-done(((bf16[1,128,64]{2,0,1:T(2,128)(2,1)}), bf16[1,128,64]{2,0,1:T(2,128)(2,1)S(1)}, u32[]{:S(2)}, u32[]{:S(2)}) %all-to-all-start.3) | async-done | bytes 16416 | tf_op jit(solution)/shard_map/all_to_all | solution.py:81
  120.3 5.7 %all-to-all-start.2 = ((bf16[128,2,128]{2,1,0:T(2,128)(2,1)}), bf16[128,2,128]{2,1,0:T(2,128)(2,1)S(1)}, u32[]{:S(2)}, u32[]{:S(2)}) async-start(bf16[128,2,128]{2,1,0:T(2,128)(2,1)} %reshape.205), calls=%async_computation.3 | async-start | bytes 131072 | tf_op jit(solution)/shard_map/all_to_all | solution.py:80
  125.9 4.4 %fusion = bf16[128,1024]{1,0:T(8,128)(2,1)} fusion(f32[128,1024]{1,0:T(8,128)S(1)} %fusion.13, bf16[128,2048]{1,0:T(8,128)(2,1)S(1)} %broadcast_multiply_fusion, bf16[1024,2048]{1,0:T(8,128)(2,1)} %param.8), kind=kOutput, calls=%fused_computation.5 | convolution fusion | flops 537133056 | bytes 5505024 | tf_op jit(solution)/shard_map/dot_general | solution.py:58
  130.3 0.1 copy.51
  130.4 0.0 copy-done.3
  130.4 0.2 convolution_bitcast_fusion.1
  130.6 0.8 copy.53
  131.4 6.1 %all-to-all-done.2 = bf16[128,2,128]{2,1,0:T(2,128)(2,1)S(1)} async-done(((bf16[128,2,128]{2,1,0:T(2,128)(2,1)}), bf16[128,2,128]{2,1,0:T(2,128)(2,1)S(1)}, u32[]{:S(2)}, u32[]{:S(2)}) %all-to-all-start.2) | async-done | bytes 65568 | tf_op jit(solution)/shard_map/all_to_all | solution.py:80
  137.6 0.1 copy.55
  137.7 1.1 convolution_bitcast_fusion
  138.8 0.0 reduce-scatter.2.cloned.1.call-done
  138.8 1.7 %fusion.2 = bf16[128,256]{1,0:T(8,128)(2,1)} fusion(bf16[32,256]{0,1:T(8,128)(2,1)S(1)} %bitcast.74, bf16[128,256]{1,0:T(8,128)(2,1)} %reduce-scatter.2.cloned.1.call-done, f32[128]{0:T(128)S(1)} %fusion.23, bf16[1,128,32]{1,2,0:T(8,128)(2,1)S(1)} %get-tuple-element.20), kind=kOutput, calls=%fused_computation.9 | convolution fusion | flops 2228224 | bytes 156160 | tf_op jit(solution)/shard_map/igu,iul->igl/dot_general | solution.py:51
  (5 shorter events, 0.1 us)
Async XLA Ops:
  7.2 22.5 %copy-start = (bf16[128,1024]{1,0:T(8,128)(2,1)S(1)}, bf16[128,1024]{1,0:T(8,128)(2,1)}, u32[]{:S(2)}) copy-start(bf16[128,1024]{1,0:T(8,128)(2,1)} %param.7) | copy-start | bytes 786436
  7.2 26.9 %copy-start.1 = (bf16[128,2048]{1,0:T(8,128)(2,1)S(1)}, bf16[128,2048]{1,0:T(8,128)(2,1)}, u32[]{:S(2)}) copy-start(bf16[128,2048]{1,0:T(8,128)(2,1)} %param.11) | copy-start | bytes 1572868
  7.2 27.0 %copy-start.2 = (bf16[512,1,8,32]{0,3,2,1:T(8,128)(2,1)S(1)}, bf16[512,1,8,32]{0,3,2,1:T(8,128)(2,1)}, u32[]{:S(2)}) copy-start(bf16[512,1,8,32]{0,3,2,1:T(8,128)(2,1)} %param.9) | copy-start | bytes 786436
  10.3 30.9 %all-to-all-start.1 = ((bf16[1,128,64]{2,0,1:T(2,128)(2,1)}), bf16[1,128,64]{2,0,1:T(2,128)(2,1)S(1)}, u32[]{:S(2)}, u32[]{:S(2)}) async-start(bf16[1,128,64]{2,0,1:T(2,128)(2,1)} %copy.42), calls=%async_computation.2 | async-start | bytes 131072 | tf_op jit(solution)/shard_map/all_to_all | solution.py:25
  29.7 109.1 %reduce-scatter.2.cloned.1.call-start = ((), (), s32[]{:S(2)}) async-start(), calls=%async_computation.5 | async-start | bytes 589824 | tf_op jit(solution)/shard_map/reduce_scatter | solution.py:45
  41.3 21.5 %all-to-all-start = ((bf16[128,2,128]{2,1,0:T(2,128)(2,1)}), bf16[128,2,128]{2,1,0:T(2,128)(2,1)S(1)}, u32[]{:S(2)}, u32[]{:S(2)}) async-start(bf16[128,2,128]{2,1,0:T(2,128)(2,1)} %reshape.203), calls=%async_computation.1 | async-start | bytes 131072 | tf_op jit(solution)/shard_map/all_to_all | solution.py:24
  95.2 35.3 %copy-start.3 = (s32[128]{0:T(128)S(1)}, s32[128]{0:T(128)}, u32[]{:S(2)}) copy-start(s32[128]{0:T(128)} %param.12) | copy-start | bytes 1540
  96.3 24.0 %all-to-all-start.3 = ((bf16[1,128,64]{2,0,1:T(2,128)(2,1)}), bf16[1,128,64]{2,0,1:T(2,128)(2,1)S(1)}, u32[]{:S(2)}, u32[]{:S(2)}) async-start(bf16[1,128,64]{2,0,1:T(2,128)(2,1)} %copy.50), calls=%async_computation.4 | async-start | bytes 131072 | tf_op jit(solution)/shard_map/all_to_all | solution.py:81
  120.3 17.3 %all-to-all-start.2 = ((bf16[128,2,128]{2,1,0:T(2,128)(2,1)}), bf16[128,2,128]{2,1,0:T(2,128)(2,1)S(1)}, u32[]{:S(2)}, u32[]{:S(2)}) async-start(bf16[128,2,128]{2,1,0:T(2,128)(2,1)} %reshape.205), calls=%async_computation.3 | async-start | bytes 131072 | tf_op jit(solution)/shard_map/all_to_all | solution.py:80
Sparse Core Ops, SparseCore 0:
  33.9 46.7 reduce-scatter.1
where the time goes:
time: 148 us; the launch traced here: 147 us
  starting transfers between devices  47.4 us (32%)
  blocking collectives  31.6 us (21%)
  waiting for transfers between devices  30.1 us (20%)
  between operations  14.9 us (10%)
  matrix products  11.9 us (8%)
  local copies, waits for them, and re-layouts  8.49 us (6%)
  other arithmetic  2.81 us (2%)
    psum x1, blocking collectives, shards(): rank_sum, back_sum = lax.psum((rank_part, back_part), 'tensor')  31.6 us
    all_to_all x1, starting transfers between devices, shards(): lax.all_to_all(up_table[ids_send], 'dp', split_axis=1, concat_axis=1, til...  19.3 us
    all_to_all x1, starting transfers between devices, shards(): lax.all_to_all(up_terms, 'dp', split_axis=1, concat_axis=1, tiled=True)  12.3 us
    all_to_all x1, waiting for transfers between devices, shards(): lax.all_to_all(down_table[ids_send], 'dp', split_axis=1, concat_axis=1, t...  11 us
    all_to_all x1, starting transfers between devices, shards(): lax.all_to_all(down_table[ids_send], 'dp', split_axis=1, concat_axis=1, t...  10.1 us
    all_to_all x1, waiting for transfers between devices, shards(): lax.all_to_all(up_terms, 'dp', split_axis=1, concat_axis=1, tiled=True)  9.16 us
    all_to_all x1, waiting for transfers between devices, shards(): lax.all_to_all(down_terms, 'dp', split_axis=1, concat_axis=1, tiled=True)  6.15 us
    all_to_all x1, starting transfers between devices, shards(): lax.all_to_all(down_terms, 'dp', split_axis=1, concat_axis=1, tiled=True)  5.67 us
  transfers between devices with their start and end apart: 5, of which 4 were waited for; matrix products, arithmetic and copies ran while one was open for 12% of the time, Pallas kernels for 0%

commit v1 on v0

v1 whole, which is shorter than its diff:
```python
import jax
import jax.numpy as jnp
from jax import lax
from jax.experimental import pallas as pl
from jax.experimental.pallas import tpu as pltpu
from jax.sharding import PartitionSpec as P

MESH = pl.DeviceIdType.MESH
BF16 = jnp.bfloat16
F32 = jnp.float32
X, Y, CORES, Z = 8, 8, 2, 8
GROUPS = X * Y * CORES
LANES = 128
NEAR = (1, 7, 2, 6)
FAR = (3, 5, 4)


def ring(step, size):
    return min(step, size - step)


OFFSETS = sorted(
    [(x, y, c) for x in range(X) for y in range(Y) for c in range(CORES) if (x, y, c) != (0, 0, 0)],
    key=lambda o: -(ring(o[0], X) + ring(o[1], Y)),
)


def nn(a, b):
    return lax.dot_general(a, b, (((1,), (0,)), ((), ())), preferred_element_type=F32)


def nt(a, b):
    return lax.dot_general(a, b, (((1,), (1,)), ((), ())), preferred_element_type=F32)


def kernel(
    rows_ref, tok_hbm, w_hbm, down_hbm, up_hbm, cot_hbm, ids_hbm,
    kv_hbm, tg_hbm, gd_hbm, gu_hbm,
    tok, w, down, up, dy, ids,
    pick, send1, recv1, send2, recv2, part, parts, chunk, chunks,
    tok_perm, tok_cols, dy_cols, dy_cols_t, frozen, back, m_down,
    kv, tg, gd, gu,
    in_sem, own_sem, a_send, a_recv, p_send, p_recv, c_send, c_recv, g_send, g_recv, out_sem,
):
    n, features = tok.shape
    rank = 32
    cols = kv.shape[1]
    adapters = down.shape[1]
    me = lax.axis_index("dp")
    col = lax.axis_index("tensor")
    mx, my, mc = me // (Y * CORES), (me // CORES) % Y, me % CORES

    loads = [
        pltpu.make_async_copy(src, dst, in_sem.at[i])
        for i, (src, dst) in enumerate(
            [(ids_hbm, ids), (down_hbm, down), (up_hbm, up), (tok_hbm, tok), (cot_hbm, dy), (w_hbm, w)]
        )
    ]
    for load in loads:
        load.start()

    def group_peer(o):
        return ((mx + o[0]) % X) * (Y * CORES) + ((my + o[1]) % Y) * CORES + (mc + o[2]) % CORES

    barrier = pltpu.get_barrier_semaphore()
    for o in OFFSETS:
        pl.semaphore_signal(barrier, inc=1, device_id=(group_peer(o), col), device_id_type=MESH)
    for i in (4, 3, 5, 2, 6, 1, 7):
        pl.semaphore_signal(barrier, inc=1, device_id=(me, (col + i) % Z), device_id_type=MESH)

    loads[0].wait()
    pairs = 2 * GROUPS
    at = lax.broadcasted_iota(jnp.int32, (pairs, GROUPS), 0) // 2
    lane = lax.broadcasted_iota(jnp.int32, (pairs, GROUPS), 1)
    own = jnp.sum(jnp.where(at == lane, ids[...].astype(F32), 0.0), axis=1, keepdims=True)
    row = lax.broadcasted_iota(jnp.int32, (pairs, adapters), 0)
    hit = lax.broadcasted_iota(jnp.int32, (pairs, adapters), 1).astype(F32) == own
    for h in range(2):
        pick[:, h * adapters:(h + 1) * adapters] = jnp.where(hit & (row % 2 == h), 1.0, 0.0).astype(BF16)
    even, odd = pick[:, :adapters], pick[:, adapters:]

    loads[1].wait()
    down_rows = nt(even, down[:LANES]) + nt(odd, down[LANES:])
    send1[0] = down_rows.astype(BF16).reshape(GROUPS, 2, LANES)
    loads[2].wait()
    up_wide = up[...].astype(F32)
    up_rows = nt(even, up_wide[:, 0, :].astype(BF16)) + nt(odd, up_wide[:, 1, :].astype(BF16))
    pad = jnp.zeros((pairs, LANES - rank), F32)
    send1[1] = jnp.concatenate([up_rows, pad], axis=1).astype(BF16).reshape(GROUPS, 2, LANES)

    pl.semaphore_wait(barrier, len(OFFSETS) + Z - 1)

    def exchange(src, dst, send_sem, recv_sem, local_sem):
        for o in OFFSETS:
            peer = group_peer(o)
            pltpu.make_async_remote_copy(
                src.at[:, peer], dst.at[:, me], send_sem, recv_sem,
                device_id=(peer, col), device_id_type=MESH,
            ).start()
        local = pltpu.make_async_copy(src.at[:, me], dst.at[:, me], local_sem)
        local.start()
        every = pltpu.make_async_remote_copy(
            src.at[:, 0:GROUPS - 1], dst.at[:, 0:GROUPS - 1], send_sem, recv_sem,
            device_id=(me, (col + 1) % Z), device_id_type=MESH,
        )
        return local, every

    local1, every1 = exchange(send1, recv1, a_send, a_recv, own_sem.at[0])

    loads[3].wait()
    loads[5].wait()

    def frozen_part(i):
        to = (col + i) % Z
        start = pl.multiple_of(to * cols, cols)
        return to, nn(tok[...], w[:, pl.ds(start, cols)])

    def send_chunk(i):
        to, value = frozen_part(i)
        chunk[i] = value.astype(BF16)
        pltpu.make_async_remote_copy(
            chunk.at[i], chunks.at[col], c_send, c_recv, device_id=(me, to), device_id_type=MESH
        ).start()

    for i in NEAR:
        send_chunk(i)

    i0 = lax.broadcasted_iota(jnp.int32, (LANES, LANES), 0)
    i1 = lax.broadcasted_iota(jnp.int32, (LANES, LANES), 1)
    order = jnp.where(i1 == (i0 % 32) * 4 + i0 // 32, 1.0, 0.0).astype(BF16)
    order_t = jnp.where(i0 == (i1 % 32) * 4 + i1 // 32, 1.0, 0.0).astype(BF16)
    blocks = features // LANES
    for k in range(blocks):
        span = slice(k * LANES, (k + 1) * LANES)
        tok_perm[:, span] = nt(tok[:, span], order).astype(BF16)
        turned = nt(order, tok[:, span]).astype(BF16)
        for j in range(4):
            tok_cols[k * 32:(k + 1) * 32, j * n:(j + 1) * n] = turned[j * 32:(j + 1) * 32]

    loads[4].wait()
    live = lax.broadcasted_iota(jnp.int32, (n, 1), 0) < rows_ref[0]
    mask = jnp.where(live, 1.0, 0.0)
    dy[...] = dy[...] * mask.astype(BF16)
    mine = pl.multiple_of(col * cols, cols)
    dy_cols[...] = dy[:, pl.ds(mine, cols)]
    dy_cols_t[...] = dy_cols[...].T
    frozen[...] = frozen_part(0)[1]

    local1.wait()
    every1.wait_recv()
    a_mat = recv1[0].reshape(pairs, LANES)
    b_mat = recv1[1].reshape(pairs, LANES)[:, :rank]
    a_tall = jnp.concatenate(
        [a_mat[k * 32:(k + 1) * 32, j * rank:(j + 1) * rank] for k in range(blocks) for j in range(4)], axis=0
    )
    sums = jnp.concatenate([nn(tok_perm[...], a_tall), nn(dy_cols[...], b_mat)], axis=1)
    half = n // 2
    part[...] = jnp.concatenate([sums[:half], sums[half:]], axis=1).astype(BF16)
    for i in (4, 3, 5, 2, 6, 1, 7):
        pltpu.make_async_remote_copy(
            part, parts.at[col], p_send, p_recv, device_id=(me, (col + i) % Z), device_id_type=MESH
        ).start()
    parts[col] = part[...]

    for i in FAR:
        send_chunk(i)
    for k in range(blocks):
        span = slice(k * LANES, (k + 1) * LANES)
        m_down[span] = nn(order_t, a_tall[span]).astype(BF16)
    wide = 256
    for k in range(features // wide):
        back[:, k * wide:(k + 1) * wide] = nt(dy[...], w[k * wide:(k + 1) * wide, :])

    every_part = pltpu.make_async_remote_copy(
        parts.at[0:Z - 1], parts.at[0:Z - 1], p_send, p_recv,
        device_id=(me, (col + 1) % Z), device_id_type=MESH,
    )
    every_part.wait_recv()
    total = parts[0].astype(F32)
    for i in range(1, Z):
        total = total + parts[i].astype(F32)
    total = total.astype(BF16)
    act = jnp.concatenate([total[:, :rank], total[:, 2 * rank:3 * rank]], axis=0)
    grad = jnp.concatenate([total[:, rank:2 * rank], total[:, 3 * rank:]], axis=0)

    grad4 = jnp.concatenate([grad] * 4, axis=1)
    place = lax.broadcasted_iota(jnp.int32, (n, LANES), 1) // rank
    spread = jnp.concatenate(
        [jnp.where(place == j, grad4, jnp.zeros_like(grad4)) for j in range(4)], axis=0
    )
    send2[0] = nn(tok_cols[...], spread).astype(BF16).reshape(GROUPS, 2, LANES)
    up_term = nn(dy_cols_t[...], act)
    send2[1] = jnp.concatenate([up_term, pad], axis=1).astype(BF16).reshape(GROUPS, 2, LANES)
    local2, every2 = exchange(send2, recv2, g_send, g_recv, own_sem.at[1])

    tg[...] = (back[...] + nt(grad, m_down[...])).astype(BF16)
    out_tg = pltpu.make_async_copy(tg, tg_hbm, out_sem.at[0])
    out_tg.start()
    every_chunk = pltpu.make_async_remote_copy(
        chunk.at[1:Z], chunks.at[0:Z - 1], c_send, c_recv,
        device_id=(me, (col + 1) % Z), device_id_type=MESH,
    )
    every_chunk.wait_recv()
    chunks[col] = jnp.zeros((n, cols), BF16)
    kv_sum = frozen[...] + nt(act, b_mat)
    for i in range(Z):
        kv_sum = kv_sum + chunks[i].astype(F32)
    kv[...] = (kv_sum * mask).astype(BF16)
    out_kv = pltpu.make_async_copy(kv, kv_hbm, out_sem.at[1])
    out_kv.start()
    every1.wait_send()
    every_part.wait_send()
    every_chunk.wait_send()

    local2.wait()
    every2.wait_recv()
    terms = jnp.concatenate(
        [recv2[0].reshape(pairs, LANES).T, recv2[1].reshape(pairs, LANES).T[:rank]], axis=0
    )
    for h in range(2):
        sums = nn(terms, pick[:, h * adapters:(h + 1) * adapters])
        gd[h * LANES:(h + 1) * LANES] = sums[:LANES]
        gu[:, h, :] = sums[LANES:]
    out_gd = pltpu.make_async_copy(gd, gd_hbm, out_sem.at[2])
    out_gu = pltpu.make_async_copy(gu, gu_hbm, out_sem.at[3])
    out_gd.start()
    out_gu.start()
    every2.wait_send()
    out_tg.wait()
    out_kv.wait()
    out_gd.wait()
    out_gu.wait()


def shards(tokens, kv_weight, adapter_down, adapter_up, cotangent, block_adapter, block_rows):
    n, features = tokens.shape
    kv_width = kv_weight.shape[1]
    adapters, _, slice_rows, rank = adapter_down.shape
    slice_cols = adapter_up.shape[3]
    cols = kv_width // Z
    down_table = adapter_down.transpose(1, 2, 3, 0).reshape(slice_rows * rank, adapters)
    up_table = adapter_up.transpose(2, 1, 3, 0).reshape(rank, slice_cols, adapters)
    ids = block_adapter.reshape(1, GROUPS)
    pairs = 2 * GROUPS
    vmem, dma = pltpu.VMEM, pltpu.SemaphoreType.DMA
    any_spec = pl.BlockSpec(memory_space=pl.ANY)
    kv, tg, gd, gu = pl.pallas_call(
        kernel,
        out_shape=[
            jax.ShapeDtypeStruct((n, cols), BF16),
            jax.ShapeDtypeStruct((n, features), BF16),
            jax.ShapeDtypeStruct((slice_rows * rank, adapters), F32),
            jax.ShapeDtypeStruct((rank, slice_cols, adapters), F32),
        ],
        in_specs=[pl.BlockSpec(memory_space=pltpu.SMEM)] + [any_spec] * 6,
        out_specs=[any_spec] * 4,
        scratch_shapes=[
            vmem((n, features), BF16),
            vmem((features, kv_width), BF16),
            vmem((slice_rows * rank, adapters), BF16),
            vmem((rank, slice_cols, adapters), BF16),
            vmem((n, kv_width), BF16),
            vmem((1, GROUPS), jnp.int32),
            vmem((pairs, 2 * adapters), BF16),
            vmem((2, GROUPS, 2, LANES), BF16),
            vmem((2, GROUPS, 2, LANES), BF16),
            vmem((2, GROUPS, 2, LANES), BF16),
            vmem((2, GROUPS, 2, LANES), BF16),
            vmem((n // 2, 4 * rank), BF16),
            vmem((Z, n // 2, 4 * rank), BF16),
            vmem((Z, n, cols), BF16),
            vmem((Z, n, cols), BF16),
            vmem((n, features), BF16),
            vmem((pairs, 4 * n), BF16),
            vmem((n, cols), BF16),
            vmem((cols, n), BF16),
            vmem((n, cols), F32),
            vmem((n, features), F32),
            vmem((features, rank), BF16),
            vmem((n, cols), BF16),
            vmem((n, features), BF16),
            vmem((slice_rows * rank, adapters), F32),
            vmem((rank, slice_cols, adapters), F32),
            dma((6,)),
            dma((2,)),
            dma, dma, dma, dma, dma, dma, dma, dma,
            dma((4,)),
        ],
        compiler_params=pltpu.CompilerParams(
            collective_id=0, has_side_effects=True, vmem_limit_bytes=40 << 20
        ),
        name="fused",
    )(block_rows, tokens, kv_weight, down_table, up_table, cotangent, ids)
    grad_down = gd.reshape(1, slice_rows, rank, adapters).transpose(3, 0, 1, 2)
    grad_up = gu.reshape(1, rank, slice_cols, adapters).transpose(3, 1, 0, 2)
    return kv, tg, grad_down, grad_up


def solution(mesh):
    return jax.shard_map(
        shards,
        mesh=mesh,
        in_specs=(
            P("dp", "tensor"),
            P("tensor", None),
            P(None, "tensor", "dp", None),
            P(None, None, "tensor", "dp"),
            P("dp", None),
            P(),
            P("dp"),
        ),
        out_specs=(
            P("dp", "tensor"),
            P("dp", "tensor"),
            P(None, "tensor", "dp", None),
            P(None, None, "tensor", "dp"),
        ),
        check_vma=False,
    )
```

time: 148 us -> 63 us (0.43)
  Pallas kernels: 0 us -> 51.9 us
  starting transfers between devices: 47.4 us -> 0 us
  blocking collectives: 31.6 us -> 0 us
  waiting for transfers between devices: 30.1 us -> 0 us
  between operations: 14.9 us -> 1.3 us
  matrix products: 11.9 us -> 0 us
  other arithmetic: 2.81 us -> 0 us
    pallas_call x0 -> x1, Pallas kernels: none -> 51.9 us  [shards(): pl.pallas_call(kernel, out_shape=[jax.ShapeDtypeStruct((n, cols), BF16),...]
    all_to_all x4 -> x0, starting transfers between devices: 47.4 us -> none  [the longest x1 19.3 us: shards(): lax.all_to_all(up_table[ids_send], 'dp', split_axis=1, concat_axis=1, til...]
    psum x1 -> x0, blocking collectives: 31.6 us -> none  [shards(): rank_sum, back_sum = lax.psum((rank_part, back_part), 'tensor')]
    all_to_all x4 -> x0, waiting for transfers between devices: 30.1 us -> none  [the longest x1 11 us: shards(): lax.all_to_all(down_table[ids_send], 'dp', split_axis=1, concat_axis=1, t...]
    dot_general x10 -> x0, matrix products: 11.9 us -> none  [the longest x1 4.41 us: shards(): lax.dot_general(dy_masked, kv_weight, (((1,), (1,)), ((), ())), preferred...]
    unnamed x14 -> x16, local copies, waits for them, and re-layouts: 2.65 us -> 9.4 us
    gather x4 -> x0, local copies, waits for them, and re-layouts: 2.34 us -> none  [the longest x2 1.39 us: shards(): up_table[ids_send]]
    reshape x5 -> x0, local copies, waits for them, and re-layouts: 2.14 us -> none  [the longest x2 1.07 us: shards(): up_table = adapter_up.reshape(n_adapters, rank_width * slice_cols)]
  transfers between devices with their start and end apart: 5 -> 0, of which waited for: 4 -> 0; matrix products, arithmetic and copies ran while one was open for 12% -> 0% of each run, Pallas kernels for 0% -> 0%
where the time goes in v1:
time: 63 us; the launch traced here: 62.6 us
  Pallas kernels  51.9 us (82%)
  local copies, waits for them, and re-layouts  9.4 us (15%)
  between operations  1.3 us (2%)
    pallas_call x1, Pallas kernels, shards(): pl.pallas_call(kernel, out_shape=[jax.ShapeDtypeStruct((n, cols), BF16),...  51.9 us
    unnamed x16, local copies, waits for them, and re-layouts  9.4 us

profile of v1, /device:TPU:1, one launch (start us, length us, event | category | flops | bytes accessed | tf_op | source)
XLA Modules:
  0.0 62.6 jit_solution(16829884533161102984)
XLA Ops:
  1.3 0.0 copy-start
  1.3 2.2 %copy-done = bf16[1024,2048]{1,0:T(8,128)(2,1)S(1)} copy-done((bf16[1024,2048]{1,0:T(8,128)(2,1)S(1)}, bf16[1024,2048]{1,0:T(8,128)(2,1)}, u32[]{:S(2)}) %copy-start) | copy-done | bytes 4194328
  3.5 0.0 copy-start.1
  3.5 1.0 %copy-done.1 = bf16[128,2048]{1,0:T(8,128)(2,1)S(1)} copy-done((bf16[128,2048]{1,0:T(8,128)(2,1)S(1)}, bf16[128,2048]{1,0:T(8,128)(2,1)}, u32[]{:S(2)}) %copy-start.1) | copy-done | bytes 524312
  4.5 0.0 copy-start.2
  4.5 0.9 %copy-done.2 = bf16[128,1024]{1,0:T(8,128)(2,1)S(1)} copy-done((bf16[128,1024]{1,0:T(8,128)(2,1)S(1)}, bf16[128,1024]{1,0:T(8,128)(2,1)}, u32[]{:S(2)}) %copy-start.2) | copy-done | bytes 262168
  5.5 0.0 copy-start.3
  5.5 0.9 %copy-done.3 = bf16[512,1,8,32]{0,3,2,1:T(8,128)(2,1)S(1)} copy-done((bf16[512,1,8,32]{0,3,2,1:T(8,128)(2,1)S(1)}, bf16[512,1,8,32]{0,3,2,1:T(8,128)(2,1)}, u32[]{:S(2)}) %copy-start.3) | copy-done | bytes 262168
  6.4 0.0 copy-start.4
  6.4 0.8 %copy-done.4 = bf16[512,32,1,2]{0,3,2,1:T(2,128)(2,1)S(1)} copy-done((bf16[512,32,1,2]{0,3,2,1:T(2,128)(2,1)S(1)}, bf16[512,32,1,2]{0,3,2,1:T(2,128)(2,1)}, u32[]{:S(2)}) %copy-start.4) | copy-done | bytes 65560
  7.3 0.0 copy-start.5
  7.3 0.7 %copy-done.5 = s32[128]{0:T(128)S(1)} copy-done((s32[128]{0:T(128)S(1)}, s32[128]{0:T(128)}, u32[]{:S(2)}) %copy-start.5) | copy-done | bytes 536
  7.9 51.9 %fused.1 = (bf16[128,256]{1,0:T(8,128)(2,1)S(1)}, bf16[128,1024]{1,0:T(8,128)(2,1)S(1)}, f32[256,512]{1,0:T(8,128)S(1)}, f32[32,2,512]{2,1,0:T(2,128)S(1)}) custom-call(s32[1]{0:T(128)S(6)} %copy.17.rows_ref, bf16[128,1024]{1,0:T(8,128)(2,1)S(1)} %copy-done.2, bf16[1024,2048]{1,0:T(8,128)(2,1)S(1)} %copy-done, bf16[256,512]{1,0:T(8,128)(2,1)S(1)} %bitcast.18, ...), custom_call_target="tpu_custom_call" | custom-call | tf_op jit(solution)/shard_map/fused/pallas_call | solution.py:247
  59.8 0.6 %copy.18 = bf16[128,256]{1,0:T(8,128)(2,1)} copy(bf16[128,256]{1,0:T(8,128)(2,1)S(1)} %get-tuple-element.20) | data formatting | bytes 131072
  60.4 0.7 %copy.19 = bf16[128,1024]{1,0:T(8,128)(2,1)} copy(bf16[128,1024]{1,0:T(8,128)(2,1)S(1)} %get-tuple-element.21) | data formatting | bytes 524288
  61.2 0.8 %copy.20 = f32[512,1,8,32]{0,3,2,1:T(8,128)} copy(f32[512,1,8,32]{0,3,2,1:T(8,128)S(1)} %bitcast.17) | data formatting | bytes 1048576
  61.9 0.7 %copy.21 = f32[512,32,1,2]{0,3,2,1:T(2,128)} copy(f32[512,32,1,2]{0,3,2,1:T(2,128)S(1)} %bitcast.19) | data formatting | bytes 262144
Async XLA Ops:
  1.3 2.2 %copy-start = (bf16[1024,2048]{1,0:T(8,128)(2,1)S(1)}, bf16[1024,2048]{1,0:T(8,128)(2,1)}, u32[]{:S(2)}) copy-start(bf16[1024,2048]{1,0:T(8,128)(2,1)} %w_hbm.1) | copy-start | bytes 12582916
  3.5 1.0 %copy-start.1 = (bf16[128,2048]{1,0:T(8,128)(2,1)S(1)}, bf16[128,2048]{1,0:T(8,128)(2,1)}, u32[]{:S(2)}) copy-start(bf16[128,2048]{1,0:T(8,128)(2,1)} %cot_hbm.1) | copy-start | bytes 1572868
  4.5 0.9 %copy-start.2 = (bf16[128,1024]{1,0:T(8,128)(2,1)S(1)}, bf16[128,1024]{1,0:T(8,128)(2,1)}, u32[]{:S(2)}) copy-start(bf16[128,1024]{1,0:T(8,128)(2,1)} %tok_hbm.1) | copy-start | bytes 786436
  5.5 0.9 %copy-start.3 = (bf16[512,1,8,32]{0,3,2,1:T(8,128)(2,1)S(1)}, bf16[512,1,8,32]{0,3,2,1:T(8,128)(2,1)}, u32[]{:S(2)}) copy-start(bf16[512,1,8,32]{0,3,2,1:T(8,128)(2,1)} %param.9) | copy-start | bytes 786436
  6.4 0.8 %copy-start.4 = (bf16[512,32,1,2]{0,3,2,1:T(2,128)(2,1)S(1)}, bf16[512,32,1,2]{0,3,2,1:T(2,128)(2,1)}, u32[]{:S(2)}) copy-start(bf16[512,32,1,2]{0,3,2,1:T(2,128)(2,1)} %param.10) | copy-start | bytes 196612
  7.3 0.7 %copy-start.5 = (s32[128]{0:T(128)S(1)}, s32[128]{0:T(128)}, u32[]{:S(2)}) copy-start(s32[128]{0:T(128)} %param.12) | copy-start | bytes 1540

commit v2 on v1

--- a/solution.py
+++ b/solution.py
@@ -23,6 +23,10 @@
     [(x, y, c) for x in range(X) for y in range(Y) for c in range(CORES) if (x, y, c) != (0, 0, 0)],
     key=lambda o: -(ring(o[0], X) + ring(o[1], Y)),
 )
+GREETINGS = sorted(
+    OFFSETS + list(range(1, Z)),
+    key=lambda o: -ring(o, Z) if isinstance(o, int) else -(ring(o[0], X) + ring(o[1], Y)),
+)
 
 
 def nn(a, b):
@@ -35,12 +39,11 @@
 
 def kernel(
     rows_ref, tok_hbm, w_hbm, down_hbm, up_hbm, cot_hbm, ids_hbm,
-    kv_hbm, tg_hbm, gd_hbm, gu_hbm,
+    kv, tg, recv2, pick,
     tok, w, down, up, dy, ids,
-    pick, send1, recv1, send2, recv2, part, parts, chunk, chunks,
+    send1, recv1, send2, part, parts, chunk, chunks,
     tok_perm, tok_cols, dy_cols, dy_cols_t, frozen, back, m_down,
-    kv, tg, gd, gu,
-    in_sem, own_sem, a_send, a_recv, p_send, p_recv, c_send, c_recv, g_send, g_recv, out_sem,
+    in_sem, own_sem, a_send, a_recv, p_send, p_recv, c_send, c_recv, g_send, g_recv,
 ):
     n, features = tok.shape
     rank = 32
@@ -63,10 +66,9 @@
         return ((mx + o[0]) % X) * (Y * CORES) + ((my + o[1]) % Y) * CORES + (mc + o[2]) % CORES
 
     barrier = pltpu.get_barrier_semaphore()
-    for o in OFFSETS:
-        pl.semaphore_signal(barrier, inc=1, device_id=(group_peer(o), col), device_id_type=MESH)
-    for i in (4, 3, 5, 2, 6, 1, 7):
-        pl.semaphore_signal(barrier, inc=1, device_id=(me, (col + i) % Z), device_id_type=MESH)
+    for o in GREETINGS:
+        to = (me, (col + o) % Z) if isinstance(o, int) else (group_peer(o), col)
+        pl.semaphore_signal(barrier, inc=1, device_id=to, device_id_type=MESH)
 
     loads[0].wait()
     pairs = 2 * GROUPS
@@ -105,11 +107,6 @@
         )
         return local, every
 
-    local1, every1 = exchange(send1, recv1, a_send, a_recv, own_sem.at[0])
-
-    loads[3].wait()
-    loads[5].wait()
-
     def frozen_part(i):
         to = (col + i) % Z
         start = pl.multiple_of(to * cols, cols)
@@ -121,6 +118,10 @@
         pltpu.make_async_remote_copy(
             chunk.at[i], chunks.at[col], c_send, c_recv, device_id=(me, to), device_id_type=MESH
         ).start()
+
+    loads[3].wait()
+    loads[5].wait()
+    local1, every1 = exchange(send1, recv1, a_send, a_recv, own_sem.at[0])
 
     for i in NEAR:
         send_chunk(i)
@@ -156,9 +157,10 @@
     sums = jnp.concatenate([nn(tok_perm[...], a_tall), nn(dy_cols[...], b_mat)], axis=1)
     half = n // 2
     part[...] = jnp.concatenate([sums[:half], sums[half:]], axis=1).astype(BF16)
-    for i in (4, 3, 5, 2, 6, 1, 7):
+    for i in range(Z - 1):
+        to = i + (i - col + Z) // Z
         pltpu.make_async_remote_copy(
-            part, parts.at[col], p_send, p_recv, device_id=(me, (col + i) % Z), device_id_type=MESH
+            part, parts.at[col], p_send, p_recv, device_id=(me, to), device_id_type=MESH
         ).start()
     parts[col] = part[...]
 
@@ -194,8 +196,6 @@
     local2, every2 = exchange(send2, recv2, g_send, g_recv, own_sem.at[1])
 
     tg[...] = (back[...] + nt(grad, m_down[...])).astype(BF16)
-    out_tg = pltpu.make_async_copy(tg, tg_hbm, out_sem.at[0])
-    out_tg.start()
     every_chunk = pltpu.make_async_remote_copy(
         chunk.at[1:Z], chunks.at[0:Z - 1], c_send, c_recv,
         device_id=(me, (col + 1) % Z), device_id_type=MESH,
@@ -206,30 +206,38 @@
     for i in range(Z):
         kv_sum = kv_sum + chunks[i].astype(F32)
     kv[...] = (kv_sum * mask).astype(BF16)
-    out_kv = pltpu.make_async_copy(kv, kv_hbm, out_sem.at[1])
-    out_kv.start()
     every1.wait_send()
     every_part.wait_send()
     every_chunk.wait_send()
 
     local2.wait()
     every2.wait_recv()
+    every2.wait_send()
+
+
+def finish(kv, tg, recv2, pick, kv_hbm, tg_hbm, gd_hbm, gu_hbm, gd, gu, sem):
+    early = [
+        pltpu.make_async_copy(src, dst, sem.at[i]) for i, (src, dst) in enumerate([(kv, kv_hbm), (tg, tg_hbm)])
+    ]
+    for copy in early:
+        copy.start()
+    pairs, adapters = pick.shape[0], pick.shape[1] // 2
+    rank = gu.shape[0]
     terms = jnp.concatenate(
         [recv2[0].reshape(pairs, LANES).T, recv2[1].reshape(pairs, LANES).T[:rank]], axis=0
     )
+    late = []
     for h in range(2):
         sums = nn(terms, pick[:, h * adapters:(h + 1) * adapters])
-        gd[h * LANES:(h + 1) * LANES] = sums[:LANES]
+        rows = pl.ds(h * LANES, LANES)
+        gd[rows] = sums[:LANES]
+        late.append(pltpu.make_async_copy(gd.at[rows], gd_hbm.at[rows], sem.at[2 + h]))
+        late[-1].start()
         gu[:, h, :] = sums[LANES:]
-    out_gd = pltpu.make_async_copy(gd, gd_hbm, out_sem.at[2])
-    out_gu = pltpu.make_async_copy(gu, gu_hbm, out_sem.at[3])
-    out_gd.start()
-    out_gu.start()
-    every2.wait_send()
-    out_tg.wait()
-    out_kv.wait()
-    out_gd.wait()
-    out_gu.wait()
+    late.append(pltpu.make_async_copy(gu, gu_hbm, sem.at[4]))
+    late[-1].start()
+    for copy in early + late:
+        copy.wait()
 
 
 def shards(tokens, kv_weight, adapter_down, adapter_up, cotangent, block_adapter, block_rows):
@@ -241,19 +249,26 @@
     down_table = adapter_down.transpose(1, 2, 3, 0).reshape(slice_rows * rank, adapters)
     up_table = adapter_up.transpose(2, 1, 3, 0).reshape(rank, slice_cols, adapters)
     ids = block_adapter.reshape(1, GROUPS)
+    operands = [
+        pltpu.with_memory_space_constraint(v, pltpu.HBM)
+        for v in (tokens, kv_weight, down_table, up_table, cotangent, ids)
+    ]
     pairs = 2 * GROUPS
     vmem, dma = pltpu.VMEM, pltpu.SemaphoreType.DMA
-    any_spec = pl.BlockSpec(memory_space=pl.ANY)
-    kv, tg, gd, gu = pl.pallas_call(
+    hbm_spec = pl.BlockSpec(memory_space=pltpu.HBM)
+    vmem_spec = pl.BlockSpec(memory_space=pltpu.VMEM)
+    kv_shape = jax.ShapeDtypeStruct((n, cols), BF16)
+    tg_shape = jax.ShapeDtypeStruct((n, features), BF16)
+    kv, tg, recv2, pick = pl.pallas_call(
         kernel,
         out_shape=[
-            jax.ShapeDtypeStruct((n, cols), BF16),
-            jax.ShapeDtypeStruct((n, features), BF16),
-            jax.ShapeDtypeStruct((slice_rows * rank, adapters), F32),
-            jax.ShapeDtypeStruct((rank, slice_cols, adapters), F32),
+            kv_shape,
+            tg_shape,
+            jax.ShapeDtypeStruct((2, GROUPS, 2, LANES), BF16),
+            jax.ShapeDtypeStruct((pairs, 2 * adapters), BF16),
         ],
-        in_specs=[pl.BlockSpec(memory_space=pltpu.SMEM)] + [any_spec] * 6,
-        out_specs=[any_spec] * 4,
+        in_specs=[pl.BlockSpec(memory_space=pltpu.SMEM)] + [hbm_spec] * 6,
+        out_specs=[vmem_spec] * 4,
         scratch_shapes=[
             vmem((n, features), BF16),
             vmem((features, kv_width), BF16),
@@ -261,8 +276,6 @@
             vmem((rank, slice_cols, adapters), BF16),
             vmem((n, kv_width), BF16),
             vmem((1, GROUPS), jnp.int32),
-            vmem((pairs, 2 * adapters), BF16),
-            vmem((2, GROUPS, 2, LANES), BF16),
             vmem((2, GROUPS, 2, LANES), BF16),
             vmem((2, GROUPS, 2, LANES), BF16),
             vmem((2, GROUPS, 2, LANES), BF16),
@@ -277,20 +290,26 @@
             vmem((n, cols), F32),
             vmem((n, features), F32),
             vmem((features, rank), BF16),
-            vmem((n, cols), BF16),
-            vmem((n, features), BF16),
-            vmem((slice_rows * rank, adapters), F32),
-            vmem((rank, slice_cols, adapters), F32),
             dma((6,)),
             dma((2,)),
             dma, dma, dma, dma, dma, dma, dma, dma,
-            dma((4,)),
         ],
         compiler_params=pltpu.CompilerParams(
             collective_id=0, has_side_effects=True, vmem_limit_bytes=40 << 20
         ),
         name="fused",
-    )(block_rows, tokens, kv_weight, down_table, up_table, cotangent, ids)
+    )(block_rows, *operands)
+    gd_shape = jax.ShapeDtypeStruct((slice_rows * rank, adapters), F32)
+    gu_shape = jax.ShapeDtypeStruct((rank, slice_cols, adapters), F32)
+    kv, tg, gd, gu = pl.pallas_call(
+        finish,
+        out_shape=[kv_shape, tg_shape, gd_shape, gu_shape],
+        in_specs=[vmem_spec] * 4,
+        out_specs=[hbm_spec] * 4,
+        scratch_shapes=[vmem(gd_shape.shape, F32), vmem(gu_shape.shape, F32), dma((5,))],
+        compiler_params=pltpu.CompilerParams(vmem_limit_bytes=16 << 20),
+        name="finish",
+    )(kv, tg, recv2, pick)
     grad_down = gd.reshape(1, slice_rows, rank, adapters).transpose(3, 0, 1, 2)
     grad_up = gu.reshape(1, rank, slice_cols, adapters).transpose(3, 1, 0, 2)
     return kv, tg, grad_down, grad_up

time: 63 us -> 48.9 us (0.78)
  local copies, waits for them, and re-layouts: 9.4 us -> 0 us
  Pallas kernels: 51.9 us -> 46.7 us
    unnamed x16 -> x0, local copies, waits for them, and re-layouts: 9.4 us -> none
    pallas_call x1 -> x2, Pallas kernels: 51.9 us -> 46.7 us  [the longest x1 45.6 us: shards(): pl.pallas_call(kernel, out_shape=[kv_shape, tg_shape, jax.ShapeDtypeStruc...]
where the time goes in v2:
time: 48.9 us; the launch traced here: 48 us
  Pallas kernels  46.7 us (96%)
  between operations  1.29 us (3%)
    pallas_call x1, Pallas kernels, shards(): pl.pallas_call(kernel, out_shape=[kv_shape, tg_shape, jax.ShapeDtypeStruc...  45.6 us
    pallas_call x1, Pallas kernels, shards(): pl.pallas_call(finish, out_shape=[kv_shape, tg_shape, gd_shape, gu_shape]...  1.1 us

profile of v2, /device:TPU:1, one launch (start us, length us, event | category | flops | bytes accessed | tf_op | source)
XLA Modules:
  0.0 48.0 jit_solution(13308396768326370693)
XLA Ops:
  1.3 45.6 %fused.1 = (bf16[128,256]{1,0:T(8,128)(2,1)S(1)}, bf16[128,1024]{1,0:T(8,128)(2,1)S(1)}, bf16[2,128,2,128]{3,2,1,0:T(2,128)(2,1)S(1)}, bf16[256,1024]{1,0:T(8,128)(2,1)S(1)}) custom-call(s32[1]{0:T(128)S(6)} %copy.13.rows_ref, bf16[128,1024]{1,0:T(8,128)(2,1)} %tok_hbm.1, bf16[1024,2048]{1,0:T(8,128)(2,1)} %w_hbm.1, bf16[256,512]{1,0:T(8,128)(2,1)} %bitcast.17, ...), custom_call_target="tpu_custom_call" | custom-call | tf_op jit(solution)/shard_map/fused/pallas_call | solution.py:262
  46.9 1.1 %finish.1 = (bf16[128,256]{1,0:T(8,128)(2,1)}, bf16[128,1024]{1,0:T(8,128)(2,1)}, f32[256,512]{1,0:T(8,128)}, f32[32,2,512]{2,1,0:T(2,128)}) custom-call(bf16[128,256]{1,0:T(8,128)(2,1)S(1)} %get-tuple-element.12.kv, bf16[128,1024]{1,0:T(8,128)(2,1)S(1)} %get-tuple-element.13.tg, bf16[2,128,2,128]{3,2,1,0:T(2,128)(2,1)S(1)} %get-tuple-element.14.recv2, ...), custom_call_target="tpu_custom_call" | custom-call | tf_op jit(solution)/shard_map/finish/pallas_call | solution.py:304

commit v3 on v2

--- a/solution.py
+++ b/solution.py
@@ -11,8 +11,7 @@
 X, Y, CORES, Z = 8, 8, 2, 8
 GROUPS = X * Y * CORES
 LANES = 128
-NEAR = (1, 7, 2, 6)
-FAR = (3, 5, 4)
+STEPS = 3
 
 
 def ring(step, size):
@@ -41,9 +40,9 @@
     rows_ref, tok_hbm, w_hbm, down_hbm, up_hbm, cot_hbm, ids_hbm,
     kv, tg, recv2, pick,
     tok, w, down, up, dy, ids,
-    send1, recv1, send2, part, parts, chunk, chunks,
+    send1, recv1, send2, part, parts, down_out, down_in, up_out, up_in, across_out, across_in,
     tok_perm, tok_cols, dy_cols, dy_cols_t, frozen, back, m_down,
-    in_sem, own_sem, a_send, a_recv, p_send, p_recv, c_send, c_recv, g_send, g_recv,
+    in_sem, own_sem, a_send, a_recv, p_send, p_recv, g_send, g_recv, d_send, d_recv, u_send, u_recv, x_send, x_recv,
 ):
     n, features = tok.shape
     rank = 32
@@ -108,23 +107,51 @@
         return local, every
 
     def frozen_part(i):
-        to = (col + i) % Z
-        start = pl.multiple_of(to * cols, cols)
-        return to, nn(tok[...], w[:, pl.ds(start, cols)])
-
-    def send_chunk(i):
-        to, value = frozen_part(i)
-        chunk[i] = value.astype(BF16)
-        pltpu.make_async_remote_copy(
-            chunk.at[i], chunks.at[col], c_send, c_recv, device_id=(me, to), device_id_type=MESH
-        ).start()
+        start = pl.multiple_of((col + i) % Z * cols, cols)
+        return nn(tok[...], w[:, pl.ds(start, cols)])
+
+    def down_copy(s):
+        return pltpu.make_async_remote_copy(
+            down_out.at[s], down_in.at[s], d_send.at[s], d_recv.at[s],
+            device_id=(me, (col + Z - 1) % Z), device_id_type=MESH,
+        )
+
+    def up_copy(s):
+        return pltpu.make_async_remote_copy(
+            up_out.at[s], up_in.at[s], u_send.at[s], u_recv.at[s],
+            device_id=(me, (col + 1) % Z), device_id_type=MESH,
+        )
+
+    def across_copy():
+        return pltpu.make_async_remote_copy(
+            across_out, across_in, x_send, x_recv, device_id=(me, (col + Z // 2) % Z), device_id_type=MESH
+        )
+
+    def ring_step(s):
+        total = frozen[Z - STEPS + s]
+        if s:
+            down_copy(s - 1).wait_recv()
+            total = total + down_in[s - 1].astype(F32)
+        down_out[s] = total.astype(BF16)
+        down_copy(s).start()
+        total = frozen[STEPS - s]
+        if s:
+            up_copy(s - 1).wait_recv()
+            total = total + up_in[s - 1].astype(F32)
+        up_out[s] = total.astype(BF16)
+        up_copy(s).start()
+
+    local1, every1 = exchange(send1, recv1, a_send, a_recv, own_sem.at[0])
 
     loads[3].wait()
     loads[5].wait()
-    local1, every1 = exchange(send1, recv1, a_send, a_recv, own_sem.at[0])
-
-    for i in NEAR:
-        send_chunk(i)
+    for i in (5, 3):
+        frozen[i] = frozen_part(i)
+    ring_step(0)
+    across_out[...] = frozen_part(4).astype(BF16)
+    across_copy().start()
+    for i in (2, 6, 1, 7, 0):
+        frozen[i] = frozen_part(i)
 
     i0 = lax.broadcasted_iota(jnp.int32, (LANES, LANES), 0)
     i1 = lax.broadcasted_iota(jnp.int32, (LANES, LANES), 1)
@@ -145,7 +172,6 @@
     mine = pl.multiple_of(col * cols, cols)
     dy_cols[...] = dy[:, pl.ds(mine, cols)]
     dy_cols_t[...] = dy_cols[...].T
-    frozen[...] = frozen_part(0)[1]
 
     local1.wait()
     every1.wait_recv()
@@ -164,8 +190,7 @@
         ).start()
     parts[col] = part[...]
 
-    for i in FAR:
-        send_chunk(i)
+    ring_step(1)
     for k in range(blocks):
         span = slice(k * LANES, (k + 1) * LANES)
         m_down[span] = nn(order_t, a_tall[span]).astype(BF16)
@@ -195,20 +220,20 @@
     send2[1] = jnp.concatenate([up_term, pad], axis=1).astype(BF16).reshape(GROUPS, 2, LANES)
     local2, every2 = exchange(send2, recv2, g_send, g_recv, own_sem.at[1])
 
+    ring_step(2)
     tg[...] = (back[...] + nt(grad, m_down[...])).astype(BF16)
-    every_chunk = pltpu.make_async_remote_copy(
-        chunk.at[1:Z], chunks.at[0:Z - 1], c_send, c_recv,
-        device_id=(me, (col + 1) % Z), device_id_type=MESH,
-    )
-    every_chunk.wait_recv()
-    chunks[col] = jnp.zeros((n, cols), BF16)
-    kv_sum = frozen[...] + nt(act, b_mat)
-    for i in range(Z):
-        kv_sum = kv_sum + chunks[i].astype(F32)
+    kv_sum = frozen[0] + nt(act, b_mat)
+    up_copy(STEPS - 1).wait_recv()
+    down_copy(STEPS - 1).wait_recv()
+    across_copy().wait_recv()
+    kv_sum = kv_sum + up_in[STEPS - 1].astype(F32) + down_in[STEPS - 1].astype(F32) + across_in[...].astype(F32)
     kv[...] = (kv_sum * mask).astype(BF16)
     every1.wait_send()
     every_part.wait_send()
-    every_chunk.wait_send()
+    for s in range(STEPS):
+        down_copy(s).wait_send()
+        up_copy(s).wait_send()
+    across_copy().wait_send()
 
     local2.wait()
     every2.wait_recv()
@@ -281,18 +306,23 @@
             vmem((2, GROUPS, 2, LANES), BF16),
             vmem((n // 2, 4 * rank), BF16),
             vmem((Z, n // 2, 4 * rank), BF16),
-            vmem((Z, n, cols), BF16),
-            vmem((Z, n, cols), BF16),
+            vmem((STEPS, n, cols), BF16),
+            vmem((STEPS, n, cols), BF16),
+            vmem((STEPS, n, cols), BF16),
+            vmem((STEPS, n, cols), BF16),
+            vmem((n, cols), BF16),
+            vmem((n, cols), BF16),
             vmem((n, features), BF16),
             vmem((pairs, 4 * n), BF16),
             vmem((n, cols), BF16),
             vmem((cols, n), BF16),
-            vmem((n, cols), F32),
+            vmem((Z, n, cols), F32),
             vmem((n, features), F32),
             vmem((features, rank), BF16),
             dma((6,)),
             dma((2,)),
-            dma, dma, dma, dma, dma, dma, dma, dma,
+            dma, dma, dma, dma, dma, dma,
+            dma((STEPS,)), dma((STEPS,)), dma((STEPS,)), dma((STEPS,)), dma, dma,
         ],
         compiler_params=pltpu.CompilerParams(
             collective_id=0, has_side_effects=True, vmem_limit_bytes=40 << 20

time: 48.9 us -> 48.1 us (0.984); the launches traced: 48 us -> 47.9 us
  no operation moved by 1% of the time
where the time goes in v3:
time: 48.1 us; the launch traced here: 47.9 us
  Pallas kernels  46.6 us (97%)
  between operations  1.29 us (3%)
    pallas_call x1, Pallas kernels, shards(): pl.pallas_call(kernel, out_shape=[kv_shape, tg_shape, jax.ShapeDtypeStruc...  45.5 us
    pallas_call x1, Pallas kernels, shards(): pl.pallas_call(finish, out_shape=[kv_shape, tg_shape, gd_shape, gu_shape]...  1.1 us

profile of v3, /device:TPU:1, one launch (start us, length us, event | category | flops | bytes accessed | tf_op | source)
XLA Modules:
  0.0 47.9 jit_solution(383324258650400574)
XLA Ops:
  1.3 45.5 %fused.1 = (bf16[128,256]{1,0:T(8,128)(2,1)S(1)}, bf16[128,1024]{1,0:T(8,128)(2,1)S(1)}, bf16[2,128,2,128]{3,2,1,0:T(2,128)(2,1)S(1)}, bf16[256,1024]{1,0:T(8,128)(2,1)S(1)}) custom-call(s32[1]{0:T(128)S(6)} %copy.13.rows_ref, bf16[128,1024]{1,0:T(8,128)(2,1)} %tok_hbm.1, bf16[1024,2048]{1,0:T(8,128)(2,1)} %w_hbm.1, bf16[256,512]{1,0:T(8,128)(2,1)} %bitcast.17, ...), custom_call_target="tpu_custom_call" | custom-call | tf_op jit(solution)/shard_map/fused/pallas_call | solution.py:287
  46.8 1.1 %finish.1 = (bf16[128,256]{1,0:T(8,128)(2,1)}, bf16[128,1024]{1,0:T(8,128)(2,1)}, f32[256,512]{1,0:T(8,128)}, f32[32,2,512]{2,1,0:T(2,128)}) custom-call(bf16[128,256]{1,0:T(8,128)(2,1)S(1)} %get-tuple-element.12.kv, bf16[128,1024]{1,0:T(8,128)(2,1)S(1)} %get-tuple-element.13.tg, bf16[2,128,2,128]{3,2,1,0:T(2,128)(2,1)S(1)} %get-tuple-element.14.recv2, ...), custom_call_target="tpu_custom_call" | custom-call | tf_op jit(solution)/shard_map/finish/pallas_call | solution.py:334
